TPU v7x, 32 devices: a whole 2x2x4 slice. The times are simulated.
32 devices in a mesh: gx: 8 (over y, x, core), gy: 4 (over z).
Axes of the slice: x: 2, y: 2, z: 4, core: 2. Of those that a mesh axis runs over, the one named last changes fastest.
Arguments:
- thermal_anomaly: float32 [32, 12, 38400], P(('gx', 'gy')), may hold values from -4 to 4
- zonal_flow_ratio: float32 [32, 12, 38400], P(('gx', 'gy')), may hold values from -0.9 to 0.9
- meridional_flow_ratio: float32 [32, 12, 38400], P(('gx', 'gy')), may hold values from -0.9 to 0.9
- diffusion_rates: float32 [32, 11, 38400], P(('gx', 'gy')), may hold values from 0.05 to 5
- ocean_bottom_scaled: float32 [32, 38400], P(('gx', 'gy')), may hold values from 0.5 to 2
- ocean_indicator: int32 [32, 38400], P(('gx', 'gy')), may hold values 0 or 1
- operator_diagonal: float32 [32, 38400], P(('gx', 'gy')), may hold values from 0.05 to 0.5
- elevation_source: float32 [32, 38400], P(('gx', 'gy')), may hold values from -32 to 32
- block_positions: int32 [32], replicated, may hold values from 0 to 31, as said below
Outputs:
- new_temp: float32 [32, 12, 38400], P(('gx', 'gy'))
- surface_height: float32 [32, 38400], P(('gx', 'gy'))
Inputs may be any that keep to these rules, and one draw needn't show every extreme that they name: `block_positions`: A permutation of 0 to 31. Tiles held by consecutive devices (the last and the first counted as consecutive) share an edge of the tile grid, which is periodic along x, except for two such pairs, 16 apart.
All inputs are finite; a program needn't handle non-finite values. No bound on the sum of `ocean_indicator` on one device may be relied on, other than what follows from the above.
Results may differ from a plain program's by a relative error of at most 0.0001.
Values sent between devices are 32-bit elements; how exact they have to be, the bound alone decides.
No kernel may reach another device: no remote copies, remote signals or barrier semaphores. Data moves between devices by JAX's collectives and lax.ppermute only.
A program may use at most 128 MiB of HBM per device.

v0:
```python
import functools

import jax
import jax.numpy as jnp
from jax import lax
from jax.experimental import pallas as pl
from jax.experimental.pallas import tpu as pltpu
from jax.sharding import PartitionSpec as P

ITERS = 4
SPAN_X = 240
SPAN_Y = 160
RIM = 4
ADVECT = 0.25
DIFFUSE = 0.12
STERIC = 0.5
LOW_RATE = 0.05
HIGH_RATE = 32.5
ROOTS = (0.02, 0.35, 0.1, 0.2)
STRETCH = 4.0
TINY = 1e-30
BOTH = ("gx", "gy")
SIDES = ((-1, 0), (1, 0), (0, -1), (0, 1), (-1, -1), (1, -1), (-1, 1), (1, 1))

LANES = 128
GROUP = 8
GROUPS = SPAN_Y // GROUP
PLANES = GROUP * SPAN_X // LANES
ROWS = GROUPS * PLANES
SLABS = GROUPS + 4
WIDE = SLABS * PLANES
START = [SPAN_X * j // LANES for j in range(GROUP)]
OFF = [SPAN_X * j % LANES for j in range(GROUP)]
LAST = [(SPAN_X * j + SPAN_X - 1) // LANES for j in range(GROUP)]
END = [(SPAN_X * j + SPAN_X - 1) % LANES for j in range(GROUP)]
FIRST_OF = [[OFF[j] for j in range(GROUP) if START[j] == a] for a in range(PLANES)]
LAST_OF = [[END[j] for j in range(GROUP) if LAST[j] == a] for a in range(PLANES)]
RIM_ROWS = 24
EDGE = 56
BUDGET = 56 * 1024 * 1024


def turn(value, shift, axis=1):
    shift = shift % value.shape[axis]
    return value if shift == 0 else pltpu.roll(value, shift, axis)


def fetching(pairs, sems):
    copies = [pltpu.make_async_copy(a, b, sems.at[n]) for n, (a, b) in enumerate(pairs)]
    for copy in copies:
        copy.start()
    return copies


def pieces_of(levels, count):
    rows = 2 * levels
    number = -(-4 * rows // count)
    runs = [[] for _ in range(4)]
    for c in range(4):
        for j in range(number):
            low, high = max(c * rows, j * count), min((c + 1) * rows, (j + 1) * count)
            if low < high:
                runs[c].append((j, low - j * count, low - c * rows, high - low))
    return number, runs


class Level:
    def __init__(self, ref, base):
        self.ref, self.base = ref, base

    def plane(self, a):
        return self.ref[comb(self.base + a), :]

    def rows(self, low, size):
        return self.ref[pl.ds(self.base + low, size), :]


def lane_of(shape):
    return lax.broadcasted_iota(jnp.int32, shape, len(shape) - 1)


def row_of(shape):
    return lax.broadcasted_iota(jnp.int32, shape, 0)


def comb(a, count=GROUPS):
    return pl.ds(a, count, stride=PLANES)


def drop(value, lanes, lane):
    for at in lanes:
        value = jnp.where(lane == at, 0.0, value)
    return value


def store_terms(a, temp, flow_x, flow_y, te, tw, tn, ts):
    spread = DIFFUSE * temp
    te[a] = spread - flow_x
    tw[a] = spread + flow_x
    tn[a, 8 : 8 + GROUPS] = spread - flow_y
    ts[a, 8 : 8 + GROUPS] = spread + flow_y


def clear_terms(tn, ts):
    none = jnp.zeros((PLANES, 1, LANES), jnp.float32)
    for ref in (tn, ts):
        ref[:, 7:8] = none
        ref[:, 8 + GROUPS : 9 + GROUPS] = none


def inner_sum(a, te, tw, tn, ts):
    lane = lane_of((GROUPS, LANES))
    here = te[a]
    east = here if a == PLANES - 1 else jnp.where(lane == 0, te[a + 1], here)
    east = drop(turn(east, -1), LAST_OF[a], lane)
    here = tw[a]
    west = here if a == 0 else jnp.where(lane == LANES - 1, tw[a - 1], here)
    west = drop(turn(west, 1), FIRST_OF[a], lane)

    def plane(ref, at):
        down = 8 + (at >= PLANES) - (at < 0)
        return ref[at % PLANES, down : down + GROUPS]

    north = turn(jnp.where(lane >= LANES - 16, plane(tn, a + 1), plane(tn, a + 2)), 16)
    south = turn(jnp.where(lane < 16, plane(ts, a - 1), plane(ts, a - 2)), -16)
    return east + west + north + south


def choose(planes, lane, get):
    value = get(planes[0])
    for j in range(1, GROUP):
        low = (OFF[j] - (32 if planes is LAST else 0)) % LANES
        value = jnp.where(jnp.logical_and(lane >= low, lane < low + 16), get(planes[j]), value)
    return value


def forcing_kernel(
    levels, per, tiles_x, tiles_y,
    pos, temp_in, zonal_in, merid_in, depth_in, ocean_in, diag_in, source_in,
    part_out, own_out, slots_out, table, around,
    temp, zonal, merid, depth, ocean, diag, source, part, own, slots,
    st, sx, sy, pt, te, tw, tn, ts, edges, holder, sems, out_sems,
):
    count = pos.shape[0]
    steps = levels // per
    number_pieces, runs = pieces_of(levels, count)
    slot = RIM_ROWS + number_pieces
    pairs = []
    for step in range(steps):
        chunk = pl.ds(step * per * ROWS, per * ROWS)
        pairs += [
            (a.at[chunk], b.at[chunk]) for a, b in ((temp_in, temp), (zonal_in, zonal), (merid_in, merid))
        ]
    pairs += [
        (a.reshape(ROWS, LANES), b)
        for a, b in ((source_in, source), (ocean_in, ocean), (depth_in, depth), (diag_in, diag))
    ]
    copies = fetching(pairs, sems)
    results = []

    def send(value, target):
        copy = pltpu.make_async_copy(value, target, out_sems.at[len(results)])
        copy.start()
        results.append(copy)

    lane = lane_of((GROUPS, LANES))
    one = lane_of((1, LANES))
    q = lane % 16
    edges[...] = jnp.zeros_like(edges)

    def number(d, carry):
        holder[pos[d]] = d
        return carry

    lax.fori_loop(0, count, number, 0)
    me = lax.axis_index("gx") * tiles_y + lax.axis_index("gy")
    here = pos[me]
    row = here // tiles_x
    column = here % tiles_x
    sides = []
    for c, (dx, dy) in enumerate(SIDES):
        there = row + dy
        inside = jnp.logical_and(there >= 0, there < tiles_y)
        target = jnp.where(inside, there, 0) * tiles_x + (column + dx + tiles_x) % tiles_x
        device = jnp.where(inside, holder[target], -1)
        table[c] = device
        sides.append(device)

    def look(y, carry):
        line = [holder[y * tiles_x + x] for x in range(tiles_x)]
        below = [holder[jnp.maximum(y - 1, 0) * tiles_x + x] for x in range(tiles_x)]
        above = [holder[jnp.minimum(y + 1, tiles_y - 1) * tiles_x + x] for x in range(tiles_x)]
        for x, device in enumerate(line):
            around[device] = line[x - 1]
            around[count + device] = line[(x + 1) % tiles_x]
            around[2 * count + device] = jnp.where(y > 0, below[x], -1)
            around[3 * count + device] = jnp.where(y < tiles_y - 1, above[x], -1)
        return carry

    lax.fori_loop(0, tiles_y, look, 0)
    clear_terms(tn, ts)

    def add(flats, low, size, fresh):
        rows = pl.ds(low, size)
        total = [None] * 3
        for t, u, v in zip(*flats):
            t = t.rows(low, size)
            new = (t, t * u.rows(low, size), t * v.rows(low, size))
            total = [b if a is None else a + b for a, b in zip(total, new)]
        for ref, value in zip((st, sx, sy), total):
            ref[rows, :] = value if fresh else ref[rows, :] + value

    for step in range(steps):
        for copy in copies[3 * step : 3 * step + 3]:
            copy.wait()
        flats = [
            [Level(ref, (step * per + n) * ROWS) for n in range(per)] for ref in (temp, zonal, merid)
        ]

        def some(m, carry):
            add(flats, pl.multiple_of(m * 8, 8), 8, step == 0)
            return carry

        lax.fori_loop(0, ROWS // 8, some, 0, unroll=4)
        if ROWS % 8:
            add(flats, ROWS - ROWS % 8, ROWS % 8, step == 0)

        for n in range(per):
            k = step * per + n
            t, u, v = (flat[n] for flat in flats)

            def term(planes, sign):
                own = choose(planes, lane, t.plane)
                flow = choose(planes, lane, u.plane)
                return DIFFUSE * own + sign * ADVECT * (flow * own)

            edges[0, 0:GROUPS] = jnp.where(q == k, turn(term(START, -1.0), k), edges[0, 0:GROUPS])
            edges[1, 0:GROUPS] = jnp.where(q == k, turn(term(LAST, 1.0), k + 17), edges[1, 0:GROUPS])
            rows = t.rows(0, 2)
            rows = DIFFUSE * rows - ADVECT * (v.rows(0, 2) * rows)
            edges[2, k : k + 1] = rows[0:1]
            edges[2, k + levels : k + levels + 1] = rows[1:2]
            rows = t.rows(ROWS - 2, 2)
            rows = DIFFUSE * rows + ADVECT * (v.rows(ROWS - 2, 2) * rows)
            edges[3, k : k + 1] = turn(jnp.where(one >= 16, rows[0:1], rows[1:2]), -16)
            edges[3, k + levels : k + levels + 1] = turn(rows[1:2], -16)

    for c in range(4):
        for j, device, low, size in runs[c]:
            slots[pl.ds(device * slot + RIM_ROWS + j, size, stride=slot), :] = edges[c, low : low + size]

    for copy in copies[3 * steps :]:
        copy.wait()

    def wet_of(rows):
        return ocean[rows, :].astype(jnp.float32)

    def masked(rows):
        return depth[rows, :] * wet_of(rows)

    for a in range(PLANES):
        total = st[comb(a), :]
        pt[a] = total
        store_terms(a, total, ADVECT * sx[comb(a), :], ADVECT * sy[comb(a), :], te, tw, tn, ts)
    for a in range(PLANES):
        total = pt[a]
        wet = wet_of(comb(a))
        change = inner_sum(a, te, tw, tn, ts) - 4.0 * DIFFUSE * total
        part[comb(a), :] = source[comb(a), :] + (STERIC / levels) * wet * (total + wet * change)
    send(part, part_out)

    def mix(values):
        value = values[4]
        for at, low in ((3, 12), (2, 11), (1, 8), (0, 4)):
            value = jnp.where(q < low, values[at], value)
        return value

    def flat(ref):
        return lambda a: ref[comb(a), :]

    def ends(planes, low):
        value = tn[planes[0], 8 : 8 + GROUPS]
        last = jnp.logical_and(lane >= low, lane < low + 16)
        return jnp.where(last, ts[planes[7], 8 : 8 + GROUPS], value)

    pack_w = mix([
        choose(START, lane, flat(part)),
        turn(choose(START, lane, lambda a: masked(comb(a))), 4),
        turn(choose(START, lane, flat(diag)), 8),
        turn(choose(START, lane, lambda a: te[a]), 11),
        turn(ends(START, OFF[7]), 12),
    ])
    pack_e = mix([
        turn(choose(LAST, lane, flat(part)), 20),
        turn(choose(LAST, lane, lambda a: masked(comb(a))), 24),
        turn(choose(LAST, lane, flat(diag)), 27),
        turn(choose(LAST, lane, lambda a: tw[a]), 28),
        turn(ends(LAST, LANES - 16), 32),
    ])
    own[0:GROUPS] = pack_w
    own[SLABS : SLABS + GROUPS] = pack_e
    north_l = tn[0, 8:9]
    north_r = tn[1, 8:9]
    south_13 = ts[PLANES - 2, 7 + GROUPS : 8 + GROUPS]
    south_14 = ts[PLANES - 1, 7 + GROUPS : 8 + GROUPS]
    south_l = turn(jnp.where(one >= 16, south_13, south_14), -16)
    south_r = turn(south_14, -16)
    own[48:49] = north_l
    own[49:50] = north_r
    own[50:51] = south_l
    own[51:52] = south_r
    send(own, own_out)
    deep = jnp.max(masked(slice(0, ROWS)), axis=(0, 1), keepdims=True)
    top = jnp.max(diag[...], axis=(0, 1), keepdims=True) + 8.0 * deep * deep
    top = jnp.broadcast_to(top, (1, LANES))

    slots[pl.ds(RIM_ROWS - 1, count, stride=slot), :] = jnp.broadcast_to(top, (count, LANES))
    eight = lane_of((8, LANES))
    eighth = row_of((8, LANES))
    for c, first, rows_l, rows_r in ((2, True, north_l, north_r), (3, False, south_l, south_r)):
        base = 0 if first else ROWS - 8
        spare = jnp.logical_and(eighth == 7, eight >= 64) if first else jnp.logical_and(eighth == 0, eight < 64)
        g = 0 if first else GROUPS - 1
        blocks = []
        block = slice(base, base + 8)
        for value, at in ((part[block, :], g), (masked(block), SLABS + g)):
            extra = jnp.broadcast_to(turn(own[at : at + 1], -16), (8, LANES))
            blocks.append(jnp.where(spare, extra, value))
        low = 0 if first else ROWS - 6
        diag_rows = diag[low : low + 6, :]
        last_row = jnp.where(one == LANES - 1, top, rows_r)

        @pl.when(sides[c] >= 0)
        def _(c=c, blocks=blocks, diag_rows=diag_rows, rows_l=rows_l, last_row=last_row):
            at = sides[c] * slot
            slots[pl.ds(at, 8), :] = blocks[0]
            slots[pl.ds(at + 8, 8), :] = blocks[1]
            slots[pl.ds(at + 16, 6), :] = diag_rows
            slots[pl.ds(at + 22, 1), :] = rows_l
            slots[pl.ds(at + 23, 1), :] = last_row

    slots[pl.ds(sides[0] * slot, GROUPS), :] = pack_w
    slots[pl.ds(sides[1] * slot, GROUPS), :] = pack_e
    for c, at in ((4, 0), (5, SLABS), (6, GROUPS - 1), (7, SLABS + GROUPS - 1)):
        @pl.when(sides[c] >= 0)
        def _(c=c, at=at):
            slots[pl.ds(sides[c] * slot, 1), :] = own[at : at + 1]
    send(slots, slots_out.reshape(count * slot, LANES))
    for copy in results:
        copy.wait()


SMEM = pl.BlockSpec(memory_space=pltpu.SMEM)


def solve_kernel(
    levels, tiles_y,
    table, around, rims, own, part, depth, ocean, diag,
    vectors, hands,
    fb, fd, fg, pw, pe, ow, oe, ed, eg, we, wn, last, rows,
):
    count = rims.shape[0]
    number_pieces, _ = pieces_of(levels, count)
    slot = RIM_ROWS + number_pieces
    share = 1 + number_pieces
    came = rims.reshape(count * slot, LANES)
    hand = hands.reshape(count * share, LANES)
    depth, ocean, diag = (ref.reshape(ROWS, LANES) for ref in (depth, ocean, diag))
    lane = lane_of((SLABS, LANES))
    slab = row_of((SLABS, LANES))
    one = lane_of((1, LANES))
    src = [table[c] for c in range(8)]

    def fetch(c, low, high):
        value = came[pl.ds(jnp.maximum(src[c], 0) * slot + low, high - low), :]
        return jnp.where(src[c] >= 0, value, 0.0)

    me = lax.axis_index("gx") * tiles_y + lax.axis_index("gy")
    for n in range(number_pieces):
        side = jnp.minimum((n * count + me) // (2 * levels), 3)
        base = (side + 1 - 2 * (side % 2)) * count

        def relay(d, carry, n=n, base=base):
            row = jnp.maximum(around[base + d], 0) * slot + RIM_ROWS + n
            hand[pl.ds(d * share + 1 + n, 1), :] = came[pl.ds(row, 1), :]
            return carry

        lax.fori_loop(0, count, relay, 0, unroll=4)

    none = jnp.zeros((WIDE - ROWS + 4, LANES), jnp.float32)
    for ref in (fb, fd, fg):
        ref[ROWS - 4 : WIDE] = none
    fb[0:ROWS] = part[...]
    fd[0:ROWS] = depth[...] * ocean[...].astype(jnp.float32)
    fg[0:ROWS] = diag[...]
    for ref, low, high in ((fb, 0, 8), (fd, 8, 16), (fg, 16, 22)):
        ref[ROWS : ROWS + high - low] = fetch(3, low, high)
        ref[WIDE - high + low : WIDE] = fetch(2, low, high)
    empty = jnp.zeros((SLABS, LANES), jnp.float32)
    for ref, side, north, south in ((pw, 0, 6, 4), (pe, 1, 7, 5)):
        ref[...] = empty
        ref[0:GROUPS] = fetch(side, 0, GROUPS)
        ref[GROUPS : GROUPS + 1] = fetch(north, 0, 1)
        ref[SLABS - 1 : SLABS] = fetch(south, 0, 1)
    for ref, at, north, south in ((ow, 0, 7, 0), (oe, SLABS, 15, 8)):
        ref[...] = empty
        ref[0:GROUPS] = own[at : at + GROUPS]
        ref[GROUPS : GROUPS + 1] = turn(fetch(3, north, north + 1), 16)
        ref[SLABS - 1 : SLABS] = turn(fetch(2, south, south + 1), 16)

    def spread(ref, j):
        a = START[j]
        first, second = ref[comb(a, SLABS), :], ref[comb(a + 1, SLABS), :]
        third = ref[comb(a + 2, SLABS), :] if a + 2 < PLANES else second
        left = turn(jnp.where(lane >= OFF[j], first, second), -OFF[j])
        right = turn(jnp.where(lane >= OFF[j], second, third), -OFF[j])
        return left, right

    def seam_row(left, right, slab_at, lanes_at):
        east = turn(pe[slab_at : slab_at + 1], 112 - lanes_at)
        west = turn(pw[slab_at : slab_at + 1], 124 - lanes_at)
        right = jnp.where(one < 112, right, jnp.where(one < 116, east, jnp.where(one >= 124, west, 0.0)))
        return jnp.broadcast_to(left, (SLABS, LANES)), jnp.broadcast_to(right, (SLABS, LANES))

    seams = {
        0: ((0, seam_row(fetch(2, 22, 23), fetch(2, 23, 24), SLABS - 1, 28)),
            (GROUPS, seam_row(own[50:51], own[51:52], GROUPS - 1, 28))),
        GROUP - 1: ((GROUPS - 1, seam_row(fetch(3, 22, 23), fetch(3, 23, 24), GROUPS, 12)),
                    (SLABS - 1, seam_row(own[48:49], own[49:50], 0, 12))),
    }
    weight = STERIC / levels
    for j in range(GROUP):
        o = OFF[j]

        def rim(right, q, width):
            east = turn(pe[...], 112 - o - q)
            west = turn(pw[...], 128 - width - o - q)
            value = jnp.where(lane < 112 + width, east, jnp.where(lane >= 128 - width, west, 0.0))
            return jnp.where(lane < 112, right, value)

        left, right = spread(fd, j)
        right = rim(right, 4, 4)
        wet_l = jnp.where(left > 0, weight, 0.0)
        wet_r = jnp.where(right > 0, weight, 0.0)
        ed[j, :, 0:LANES] = left
        ed[j, :, LANES:] = right
        left, right = spread(fg, j)
        eg[j, :, 0:LANES] = left
        eg[j, :, LANES:] = rim(right, 8, 3)
        left, right = spread(fb, j)
        right = rim(right, 0, 4)
        seam_l = jnp.where(lane == 0, turn(pw[...], -o - 11), 0.0)
        seam_r = jnp.where(lane == 127, turn(ow[...], 127 - o - 11), 0.0)
        seam_r = jnp.where(lane == 111, turn(pe[...], 111 - o - 11), seam_r)
        seam_r = jnp.where(lane == 112, turn(oe[...], 112 - o - 11), seam_r)
        for at, (row_l, row_r) in seams.get(j, ()):
            seam_l = seam_l + jnp.where(slab == at, row_l, 0.0)
            seam_r = seam_r + jnp.where(slab == at, row_r, 0.0)
        vectors[0, j, :, 0:LANES] = left + wet_l * seam_l
        vectors[0, j, :, LANES:] = right + wet_r * seam_r

    for j in range(GROUP):
        d = ed[j]
        we[j] = d * turn(d, -1)
        above = ed[j + 1] if j < GROUP - 1 else turn(ed[0], -1, 0)
        wn[j] = d * above

    top = jnp.max(came[pl.ds(RIM_ROWS - 1, count, stride=slot), :], axis=0, keepdims=True)
    top = jnp.max(jnp.where(one == LANES - 1, top, 0.0), axis=1, keepdims=True)
    scale = STRETCH / top

    big = (SLABS, 2 * LANES)
    mine = jnp.logical_and(row_of(big) < GROUPS, lane_of(big) < SPAN_X)
    pair = 0
    for k in range(5):
        sums = [None] * (k + 1)
        new = last if k == 4 else vectors.at[k]
        if k:
            v = vectors.at[k - 1]
            flow_below = wn[GROUP - 1] * (v[GROUP - 1] - turn(v[0], -1, 0))
            flow_below = turn(flow_below, 1, 0)
        for j in range(GROUP):
            if k:
                here = v[j]
                above = v[j + 1] if j < GROUP - 1 else turn(v[0], -1, 0)
                flow_x = we[j] * (here - turn(here, -1))
                flow_y = wn[j] * (here - above)
                image = eg[j] * here + (flow_x - turn(flow_x, 1)) + (flow_y - flow_below)
                fresh = scale * image - (STRETCH * ROOTS[k - 1]) * here
                flow_below = flow_y
                new[j] = fresh
            else:
                fresh = new[j]
            held = jnp.where(mine, fresh, 0.0)
            for i in range(k + 1):
                other = vectors[i, j] if i < k else held
                value = held * other
                sums[i] = value if sums[i] is None else sums[i] + value
        for i in range(k + 1):
            rows[pair : pair + 1] = jnp.sum(sums[i][:, 0:LANES] + sums[i][:, LANES:], axis=0, keepdims=True)
            pair += 1
    rows[pair : pair + 1] = jnp.where(one == 0, top, 0.0)
    total = jnp.sum(rows[...], axis=1, keepdims=True)
    spot = row_of((16, LANES)) == lane_of((16, LANES))
    line = jnp.sum(jnp.where(spot, total, 0.0), axis=0, keepdims=True)
    hand[pl.ds(0, count, stride=share), :] = jnp.broadcast_to(line, (count, LANES))


def finish_kernel(
    levels, per, table, hands, vectors, edges, inner_in, tracer_out, surface_out,
    cells, flat, left, right, message, sems, out_sems,
):
    count = hands.shape[0]
    number_pieces, runs = pieces_of(levels, count)
    share = 1 + number_pieces
    came = hands.reshape(count * share, LANES)
    steps = levels // per
    chunks = [pl.ds(step * per * ROWS, per * ROWS) for step in range(steps)]
    copies = fetching([(inner_in.at[c], cells.at[c]) for c in chunks], sems)
    row = jnp.sum(came[pl.ds(0, count, stride=share), :], axis=0, keepdims=True)
    one = lane_of((1, LANES))
    entry = {}
    pair = 0
    for k in range(5):
        for i in range(k + 1):
            value = jnp.sum(jnp.where(one == pair, row, 0.0), axis=1, keepdims=True)
            entry[i, k] = entry[k, i] = value
            pair += 1
    top = jnp.sum(jnp.where(one == pair, row, 0.0), axis=1, keepdims=True) * (1.0 / count)

    def image(c):
        out = [None] * 5
        for k in range(4):
            if c[k] is None:
                continue
            low = ROOTS[k] * c[k]
            out[k] = low if out[k] is None else out[k] + low
            out[k + 1] = (1.0 / STRETCH) * c[k]
        return out

    def dot(a, b):
        total = None
        for i in range(5):
            if a[i] is None:
                continue
            inner = None
            for j in range(5):
                if b[j] is not None:
                    value = entry[i, j] * b[j]
                    inner = value if inner is None else inner + value
            total = a[i] * inner if total is None else total + a[i] * inner
        return total

    def axpy(a, s, b):
        return [
            x if y is None else (s * y if x is None else x + s * y) for x, y in zip(a, b)
        ]

    r = [jnp.ones((1, 1), jnp.float32)] + [None] * 4
    p = list(r)
    x = [None] * 5
    rr = entry[0, 0]
    for n in range(ITERS):
        q = image(p)
        step = rr / jnp.maximum(dot(p, q), TINY)
        step = jnp.clip(step, top * (1.0 / HIGH_RATE), top * (1.0 / LOW_RATE))
        x = axpy(x, step, p)
        if n < ITERS - 1:
            r = axpy(r, -step, q)
            fresh = jnp.maximum(dot(r, r), 0.0)
            p = axpy(r, fresh / jnp.maximum(rr, TINY), p)
            rr = fresh
    factors = [c / top for c in x[:4]]
    for j in range(GROUP):
        value = None
        for k in range(4):
            term = factors[k] * vectors[k, j]
            value = term if value is None else value + term
        left[j] = turn(value[:, 0:LANES], OFF[j])
        right[j] = turn(value[:, LANES:], OFF[j])
    lane = lane_of((SLABS, LANES))
    for a in range(PLANES):
        value = None
        for j in range(GROUP):
            for half, ref in ((0, left), (1, right)):
                low = max(SPAN_X * j + LANES * half - LANES * a, 0)
                high = min(SPAN_X * j + (LANES if half == 0 else SPAN_X) - LANES * a, LANES)
                if low >= high:
                    continue
                value = ref[j] if value is None else jnp.where(lane >= low, ref[j], value)
        flat[comb(a), :] = value[0:GROUPS]
    results = [pltpu.make_async_copy(flat, surface_out.reshape(ROWS, LANES), out_sems.at[0])]
    results[0].start()

    for c in range(4):
        for j, device, low, size in runs[c ^ 1]:
            value = came[pl.ds(device * share + 1 + j, size, stride=share), :]
            message[c, low : low + size] = jnp.where(table[c] >= 0, value, 0.0)
    sums = []
    for k in range(levels):
        value = edges[2 * levels - 1] * jnp.concatenate([
            turn(message[0], -k), turn(message[1], -k),
            message[2, k : k + 1], message[2, k + levels : k + levels + 1],
            message[3, k : k + 1], message[3, k + levels : k + levels + 1],
            jnp.zeros((4, LANES), jnp.float32),
        ], axis=0)
        if k:
            value = value + edges[2 * levels + k - 1] * sums[-1]
        sums.append(value * edges[levels - 1 + k])
    for k in range(levels - 2, -1, -1):
        sums[k] = sums[k] + edges[k] * sums[k + 1]
    lane = lane_of((GROUPS, LANES))
    slab = row_of((GROUPS, LANES))
    for k in range(levels):
        if k % per == 0:
            copies[k // per].wait()
        west = sums[k][0:GROUPS]
        east = turn(sums[k][SLABS : SLABS + GROUPS], -17)
        south_l, south_r = sums[k][48:49], sums[k][49:50]
        north_l, north_r = turn(sums[k][50:51], 16), turn(sums[k][51:52], 16)
        for a in range(PLANES):
            rim = None
            for at, source in [(at, west) for at in FIRST_OF[a]] + [(at, east) for at in LAST_OF[a]]:
                rim = jnp.where(lane == at, source, 0.0 if rim is None else rim)
            if rim is None:
                continue
            if a == 0:
                rim = rim + jnp.where(slab == 0, south_l, 0.0)
            if a == 1:
                rim = rim + jnp.where(jnp.logical_and(slab == 0, lane < 112), south_r, 0.0)
            if a == PLANES - 2:
                rim = rim + jnp.where(jnp.logical_and(slab == GROUPS - 1, lane >= 16), north_l, 0.0)
            if a == PLANES - 1:
                rim = rim + jnp.where(slab == GROUPS - 1, jnp.where(lane < 16, north_l, north_r), 0.0)
            rows = comb(k * ROWS + a)
            cells[rows, :] = cells[rows, :] + rim
        if k % per == per - 1:
            step = k // per
            copy = pltpu.make_async_copy(
                cells.at[chunks[step]], tracer_out.at[chunks[step]], out_sems.at[1 + step]
            )
            copy.start()
            results.append(copy)
    for copy in results:
        copy.wait()


def tracer_kernel(
    levels, per, temp_in, zonal_in, merid_in, rates_in, ocean_in,
    inner_out, edges_out,
    temp, zonal, merid, rates, ocean, out, edges,
    te, tw, tn, ts, stepped, border, sems, out_sems,
):
    steps = levels // per
    pairs = [(ocean_in.reshape(ROWS, LANES), ocean)]
    for step in range(steps):
        chunk = pl.ds(step * per * ROWS, per * ROWS)
        pairs += [
            (a.at[chunk], b.at[chunk]) for a, b in ((temp_in, temp), (zonal_in, zonal), (merid_in, merid))
        ]
    copies = fetching(pairs + [(rates_in.reshape((levels - 1) * ROWS, LANES), rates)], sems)
    lane = lane_of((GROUPS, LANES))
    one = lane_of((1, LANES))
    clear_terms(tn, ts)

    copies[0].wait()
    for step in range(steps):
        for copy in copies[1 + 3 * step : 4 + 3 * step]:
            copy.wait()

        def level(k, carry):
            t, u, v = (Level(ref, k * ROWS) for ref in (temp, zonal, merid))
            for a in range(PLANES):
                own = t.plane(a)
                quarter = ADVECT * own
                store_terms(a, own, u.plane(a) * quarter, v.plane(a) * quarter, te, tw, tn, ts)
            for a in range(PLANES):
                own = t.plane(a)
                change = inner_sum(a, te, tw, tn, ts) - 4.0 * DIFFUSE * own
                stepped[k, a] = own + ocean[comb(a), :].astype(jnp.float32) * change
            return carry

        lax.fori_loop(step * per, step * per + per, level, 0)
    copies[-1].wait()

    def block(a, carry):
        for low in range(0, GROUPS, 8):
            size = min(8, GROUPS - low)

            def rows(k):
                return pl.ds(k * ROWS + low * PLANES + a, size, stride=PLANES)

            gains = []
            sums = []
            for k in range(levels):
                value = stepped[k, a, low : low + size]
                pivot = 1.0
                if k > 0:
                    pivot = pivot + upper - upper * gains[-1]
                    value = value + upper * sums[-1]
                if k < levels - 1:
                    lower = rates[rows(k), :]
                    inverse = 1.0 / (pivot + lower)
                    gains.append(lower * inverse)
                    upper = lower
                else:
                    inverse = 1.0 / pivot
                sums.append(value * inverse)
            result = sums[-1]
            out[rows(levels - 1), :] = result
            for k in range(levels - 2, -1, -1):
                result = sums[k] + gains[k] * result
                out[rows(k), :] = result
        return carry

    lax.fori_loop(0, PLANES, block, 0)

    def edge(ref, base, at):
        def get(a):
            return ref[comb(base + a), :].astype(jnp.float32)

        border[0:GROUPS] = choose(START, lane, get)
        border[SLABS : SLABS + GROUPS] = turn(choose(LAST, lane, get), 17)
        border[48:50] = ref[base : base + 2, :].astype(jnp.float32)
        rows = ref[base + ROWS - 2 : base + ROWS, :].astype(jnp.float32)
        border[50:51] = turn(jnp.where(one >= 16, rows[0:1], rows[1:2]), -16)
        border[51:52] = turn(rows[1:2], -16)
        edges[at] = border[...]

    border[...] = jnp.zeros_like(border)
    edge(ocean, 0, 2 * levels - 1)
    gain = None
    for k in range(levels):
        pivot = 1.0
        if k > 0:
            upper = edges[2 * levels + k - 1]
            pivot = pivot + upper - upper * gain
        if k < levels - 1:
            edge(rates, k * ROWS, 2 * levels + k)
            lower = edges[2 * levels + k]
            inverse = 1.0 / (pivot + lower)
            gain = lower * inverse
            edges[k] = gain
        else:
            inverse = 1.0 / pivot
        edges[levels - 1 + k] = inverse
        if k == 0:
            results = fetching([(out, inner_out)], out_sems)
    results.append(pltpu.make_async_copy(edges, edges_out, out_sems.at[1]))
    results[-1].start()
    for copy in results:
        copy.wait()


def on_device(
    thermal_anomaly,
    zonal_flow_ratio,
    meridional_flow_ratio,
    diffusion_rates,
    ocean_bottom_scaled,
    ocean_indicator,
    operator_diagonal,
    elevation_source,
    block_positions,
):
    levels, cells = thermal_anomaly.shape[1:]
    nx = lax.axis_size("gx")
    ny = lax.axis_size("gy")
    count = block_positions.shape[0]
    planes = (ocean_bottom_scaled, ocean_indicator, operator_diagonal, elevation_source)
    depth, ocean, diag, source = planes
    f32 = jnp.float32
    per = next(n for n in (4, 2, 6, levels) if levels % n == 0 and n * ROWS % 8 == 0)
    steps = levels // per
    large = pltpu.CompilerParams(vmem_limit_bytes=BUDGET)
    small = pltpu.CompilerParams(vmem_limit_bytes=BUDGET // 3)
    temp, zonal, merid = (
        array.reshape(levels * ROWS, LANES)
        for array in (thermal_anomaly, zonal_flow_ratio, meridional_flow_ratio)
    )
    rates = diffusion_rates.reshape(levels - 1, 1, cells)
    hbm = pl.BlockSpec(memory_space=pltpu.HBM)
    here = pl.BlockSpec(memory_space=pltpu.VMEM)

    def vmem(*shape, kind=f32):
        return pltpu.VMEM(shape, kind)

    def out(*shape, kind=f32):
        return jax.ShapeDtypeStruct(shape, kind)

    def sems(number):
        return pltpu.SemaphoreType.DMA((number,))

    deep = vmem(levels * ROWS, LANES)
    flat = vmem(ROWS, LANES)
    flat_int = vmem(ROWS, LANES, kind=jnp.int32)
    plane = vmem(PLANES, GROUPS, LANES)
    tall = vmem(PLANES, 40, LANES)
    numbers = pltpu.SMEM((count,), jnp.int32)
    number_pieces, _ = pieces_of(levels, count)
    slot = RIM_ROWS + number_pieces
    share = 1 + number_pieces
    part, own, slots, table, around = pl.pallas_call(
        functools.partial(forcing_kernel, levels, per, nx, ny),
        in_specs=[SMEM] + [hbm] * 7,
        out_specs=[hbm] * 3 + [SMEM] * 2,
        out_shape=[
            out(ROWS, LANES), out(56, LANES), out(count, 1, slot * LANES),
            out(8, kind=jnp.int32), out(4 * count, kind=jnp.int32),
        ],
        scratch_shapes=[deep] * 3 + [flat, flat_int, flat, flat]
        + [flat, vmem(56, LANES), vmem(count * slot, LANES)]
        + [flat] * 3 + [plane] * 3 + [tall] * 2
        + [vmem(4, 2 * levels, LANES), numbers, sems(3 * steps + 4), sems(3)],
        compiler_params=large,
        name="forcing",
    )(block_positions, temp, zonal, merid, depth, ocean, diag, source)
    rims = lax.all_to_all(slots, BOTH, 0, 0, tiled=True)

    inner, edges = pl.pallas_call(
        functools.partial(tracer_kernel, levels, per),
        in_specs=[hbm] * 5,
        out_specs=[hbm] * 2,
        out_shape=[out(levels * ROWS, LANES), out(3 * levels - 1, EDGE, LANES)],
        scratch_shapes=[deep] * 3 + [vmem((levels - 1) * ROWS, LANES), flat_int, deep]
        + [vmem(3 * levels - 1, EDGE, LANES)]
        + [plane] * 2 + [tall] * 2
        + [vmem(levels, PLANES, GROUPS, LANES), vmem(EDGE, LANES), sems(3 * steps + 2), sems(2)],
        compiler_params=large,
        name="tracer",
    )(temp, zonal, merid, rates, ocean)

    rims, edges = lax.optimization_barrier((rims, edges))
    extended = vmem(GROUP, SLABS, 2 * LANES)
    vectors, hand = pl.pallas_call(
        functools.partial(solve_kernel, levels, ny),
        in_specs=[SMEM, SMEM] + [here] * 6,
        out_specs=[here] * 2,
        out_shape=[out(4, GROUP, SLABS, 2 * LANES), out(count, 1, share * LANES)],
        scratch_shapes=[vmem(WIDE, LANES)] * 3 + [vmem(SLABS, LANES)] * 4 + [extended] * 5 + [vmem(16, LANES)],
        compiler_params=small,
        name="vectors",
    )(table, around, rims, own, part, depth, ocean, diag)
    hands = lax.all_to_all(hand, BOTH, 0, 0, tiled=True)

    new_temp, surface = pl.pallas_call(
        functools.partial(finish_kernel, levels, per),
        in_specs=[SMEM] + [here] * 3 + [hbm],
        out_specs=[hbm] * 2,
        out_shape=[out(levels * ROWS, LANES), out(1, cells)],
        input_output_aliases={4: 0},
        scratch_shapes=[
            deep, flat, vmem(GROUP, SLABS, LANES), vmem(GROUP, SLABS, LANES), vmem(4, 2 * levels, LANES),
            sems(steps), sems(1 + steps),
        ],
        compiler_params=small,
        name="finish",
    )(table, hands, vectors, edges, inner)
    return new_temp.reshape(1, levels, cells), surface


def solution(mesh):
    deep = P(BOTH, None, None)
    flat = P(BOTH, None)
    return jax.shard_map(
        on_device,
        mesh=mesh,
        in_specs=(deep, deep, deep, deep, flat, flat, flat, flat, P()),
        out_specs=(deep, flat),
        check_vma=False,
    )
```

profile of v0, /device:TPU:0, one launch (start us, length us, event | category | flops | bytes accessed | tf_op | source)
XLA Modules:
  0.0 43.1 jit_solution(16099789217071829350)
XLA Ops:
  0.6 5.5 %forcing.1 = (f32[300,128]{1,0:T(8,128)}, f32[56,128]{1,0:T(8,128)}, f32[32,1,3456]{2,1,0:T(1,128)}, s32[8]{0:T(128)}, s32[128]{0:T(128)}) custom-call(s32[32]{0:T(128)} %pos.1, f32[3600,128]{1,0:T(8,128)} %bitcast.5, f32[3600,128]{1,0:T(8,128)} %bitcast.7, f32[3600,128]{1,0:T(8,128)} %bitcast.9, f32[1,38400]{1,0:T(1,128)} %depth.1, s32[1,38400]{1,0:T(1,128)} %ocean.1, ...), custom_call_target="tpu_custom_call" | custom-call | tf_op jit(solution)/shard_map/forcing/pallas_call | solution.py:803
  6.1 7.3 %all-to-all-start = ((f32[32,1,3456]{2,1,0:T(1,128)}), f32[32,1,3456]{2,1,0:T(1,128)S(1)}, u32[]{:S(2)}, u32[]{:S(2)}) async-start(f32[32,1,3456]{2,1,0:T(1,128)} %get-tuple-element.17), calls=%async_computation | async-start | bytes 884736 | tf_op jit(solution)/shard_map/all_to_all | solution.py:818
  13.4 0.0 copy-start
  13.4 0.0 copy-start.2
  13.4 0.0 copy-start.3
  13.5 0.0 copy-start.4
  13.5 0.0 copy-start.5
  13.5 0.0 copy-start.6
  13.5 0.0 copy-start.7
  13.5 9.0 %tracer.1 = (f32[3600,128]{1,0:T(8,128)}, f32[35,56,128]{2,1,0:T(8,128)}) custom-call(f32[3600,128]{1,0:T(8,128)} %bitcast.6, f32[3600,128]{1,0:T(8,128)} %bitcast.8, f32[3600,128]{1,0:T(8,128)} %bitcast.10, f32[11,1,38400]{2,1,0:T(1,128)} %bitcast.12, s32[1,38400]{1,0:T(1,128)} %ocean.1), custom_call_target="tpu_custom_call" | custom-call | tf_op jit(solution)/shard_map/tracer/pallas_call | solution.py:820
  22.5 0.0 copy-start.1
  22.5 3.7 %all-to-all-done.rims = f32[32,1,3456]{2,1,0:T(1,128)S(1)} async-done(((f32[32,1,3456]{2,1,0:T(1,128)}), f32[32,1,3456]{2,1,0:T(1,128)S(1)}, u32[]{:S(2)}, u32[]{:S(2)}) %all-to-all-start) | async-done | bytes 442400 | tf_op jit(solution)/shard_map/all_to_all | solution.py:818
  26.2 0.0 copy-done
  26.2 0.0 copy-done.2
  26.2 0.0 copy-done.3
  26.2 0.0 copy-done.4
  26.2 0.0 copy-done.5
  26.2 0.0 copy-done.6
  26.2 0.0 copy-done.7
  26.3 2.5 %vectors.1 = (f32[4,8,24,256]{3,2,1,0:T(8,128)S(1)}, f32[32,1,512]{2,1,0:T(1,128)S(1)}) custom-call(s32[8]{0:T(128)S(1)} %copy-done.6, s32[128]{0:T(128)S(1)} %copy-done.7, f32[32,1,3456]{2,1,0:T(1,128)S(1)} %all-to-all-done.rims, f32[56,128]{1,0:T(8,128)S(1)} %copy-done.5, f32[300,128]{1,0:T(8,128)S(1)} %copy-done.4, f32[1,38400]{1,0:T(1,128)S(1)} %copy-done.2, ...), custom_call_target="tpu_custom_call" | custom-call | tf_op jit(solution)/shard_map/vectors/pallas_call | solution.py:835
  28.8 11.2 %all_to_all.10.hands = f32[32,1,512]{2,1,0:T(1,128)S(1)} all-to-all(f32[32,1,512]{2,1,0:T(1,128)S(1)} %get-tuple-element.22), channel_id=1, replica_groups=mesh['gx'=8,'gy'=4] {'gx','gy'}, dimensions={0} | all-to-all | bytes 131072 | tf_op jit(solution)/shard_map/all_to_all | solution.py:844
  40.0 0.0 copy-done.1
  40.0 3.1 %finish.1 = (f32[3600,128]{1,0:T(8,128)}, f32[1,38400]{1,0:T(1,128)}) custom-call(s32[8]{0:T(128)S(1)} %copy-done.6, f32[32,1,512]{2,1,0:T(1,128)S(1)} %all_to_all.10.hands, f32[4,8,24,256]{3,2,1,0:T(8,128)S(1)} %get-tuple-element.23.vectors, f32[35,56,128]{2,1,0:T(8,128)S(1)} %copy-done.1, ...), custom_call_target="tpu_custom_call", output_to_operand_aliasing={{0}: (4, {})} | custom-call | tf_op jit(solution)/shard_map/finish/pallas_call | solution.py:846
Async XLA Ops:
  6.1 20.1 %all-to-all-start = ((f32[32,1,3456]{2,1,0:T(1,128)}), f32[32,1,3456]{2,1,0:T(1,128)S(1)}, u32[]{:S(2)}, u32[]{:S(2)}) async-start(f32[32,1,3456]{2,1,0:T(1,128)} %get-tuple-element.17), calls=%async_computation | async-start | bytes 884736 | tf_op jit(solution)/shard_map/all_to_all | solution.py:818
  13.4 12.8 %copy-start = (s32[1,38400]{1,0:T(1,128)S(1)}, s32[1,38400]{1,0:T(1,128)}, u32[]{:S(2)}) copy-start(s32[1,38400]{1,0:T(1,128)} %ocean.1) | copy-start | bytes 460804
  13.4 12.8 %copy-start.2 = (f32[1,38400]{1,0:T(1,128)S(1)}, f32[1,38400]{1,0:T(1,128)}, u32[]{:S(2)}) copy-start(f32[1,38400]{1,0:T(1,128)} %depth.1) | copy-start | bytes 460804
  13.4 12.8 %copy-start.3 = (f32[1,38400]{1,0:T(1,128)S(1)}, f32[1,38400]{1,0:T(1,128)}, u32[]{:S(2)}) copy-start(f32[1,38400]{1,0:T(1,128)} %diag.1) | copy-start | bytes 460804
  13.5 12.8 %copy-start.4 = (f32[300,128]{1,0:T(8,128)S(1)}, f32[300,128]{1,0:T(8,128)}, u32[]{:S(2)}) copy-start(f32[300,128]{1,0:T(8,128)} %get-tuple-element.21.part) | copy-start | bytes 460804
  13.5 12.8 %copy-start.5 = (f32[56,128]{1,0:T(8,128)S(1)}, f32[56,128]{1,0:T(8,128)}, u32[]{:S(2)}) copy-start(f32[56,128]{1,0:T(8,128)} %get-tuple-element.20.own) | copy-start | bytes 86020
  13.5 12.8 %copy-start.6 = (s32[8]{0:T(128)S(1)}, s32[8]{0:T(128)}, u32[]{:S(2)}) copy-start(s32[8]{0:T(128)} %get-tuple-element.15.table) | copy-start | bytes 100
  13.5 12.8 %copy-start.7 = (s32[128]{0:T(128)S(1)}, s32[128]{0:T(128)}, u32[]{:S(2)}) copy-start(s32[128]{0:T(128)} %get-tuple-element.16.around) | copy-start | bytes 1540
  22.5 17.5 %copy-start.1 = (f32[35,56,128]{2,1,0:T(8,128)S(1)}, f32[35,56,128]{2,1,0:T(8,128)}, u32[]{:S(2)}) copy-start(f32[35,56,128]{2,1,0:T(8,128)} %get-tuple-element.24.edges) | copy-start | bytes 3010564
where the time goes:
time: 43.4 us; the launch traced here: 43.1 us
  Pallas kernels  20.1 us (46%)
  blocking collectives  11.2 us (26%)
  starting transfers between devices  7.31 us (17%)
  waiting for transfers between devices  3.67 us (8%)
  between operations  0.75 us (2%)
    all_to_all x1, blocking collectives, on_device(): hands = lax.all_to_all(hand, BOTH, 0, 0, tiled=True)  11.2 us
    pallas_call x1, Pallas kernels, on_device(): pl.pallas_call(functools.partial(tracer_kernel, levels, per), in_specs=[h...  9.01 us
    all_to_all x1, starting transfers between devices, on_device(): rims = lax.all_to_all(slots, BOTH, 0, 0, tiled=True)  7.31 us
    pallas_call x1, Pallas kernels, on_device(): pl.pallas_call(functools.partial(forcing_kernel, levels, per, nx, ny), in...  5.47 us
    all_to_all x1, waiting for transfers between devices, on_device(): rims = lax.all_to_all(slots, BOTH, 0, 0, tiled=True)  3.67 us
    pallas_call x1, Pallas kernels, on_device(): pl.pallas_call(functools.partial(finish_kernel, levels, per), in_specs=[S...  3.12 us
    pallas_call x1, Pallas kernels, on_device(): pl.pallas_call(functools.partial(solve_kernel, levels, ny), in_specs=[SME...  2.53 us
  transfers between devices with their start and end apart: 1, of which 1 were waited for; matrix products, arithmetic and copies ran while one was open for 0% of the time, Pallas kernels for 21%

commit v1 on v0

--- a/solution.py
+++ b/solution.py
@@ -36,7 +36,7 @@
 FIRST_OF = [[OFF[j] for j in range(GROUP) if START[j] == a] for a in range(PLANES)]
 LAST_OF = [[END[j] for j in range(GROUP) if LAST[j] == a] for a in range(PLANES)]
 RIM_ROWS = 24
-EDGE = 56
+EDGE = 32
 BUDGET = 56 * 1024 * 1024
 
 
@@ -507,8 +507,8 @@
 
 
 def finish_kernel(
-    levels, per, table, hands, vectors, edges, inner_in, tracer_out, surface_out,
-    cells, flat, left, right, message, sems, out_sems,
+    levels, per, table, hands, vectors, edges, inner, tracer_out, surface_out,
+    cells, flat, left, right, message, out_sems,
 ):
     count = hands.shape[0]
     number_pieces, runs = pieces_of(levels, count)
@@ -516,7 +516,6 @@
     came = hands.reshape(count * share, LANES)
     steps = levels // per
     chunks = [pl.ds(step * per * ROWS, per * ROWS) for step in range(steps)]
-    copies = fetching([(inner_in.at[c], cells.at[c]) for c in chunks], sems)
     row = jnp.sum(came[pl.ds(0, count, stride=share), :], axis=0, keepdims=True)
     one = lane_of((1, LANES))
     entry = {}
@@ -596,13 +595,14 @@
         for j, device, low, size in runs[c ^ 1]:
             value = came[pl.ds(device * share + 1 + j, size, stride=share), :]
             message[c, low : low + size] = jnp.where(table[c] >= 0, value, 0.0)
+    second = lane_of((SLABS, LANES)) % 16 == 1
     sums = []
     for k in range(levels):
         value = edges[2 * levels - 1] * jnp.concatenate([
-            turn(message[0], -k), turn(message[1], -k),
+            jnp.where(second, turn(message[1], 1 - k), turn(message[0], -k)),
             message[2, k : k + 1], message[2, k + levels : k + levels + 1],
             message[3, k : k + 1], message[3, k + levels : k + levels + 1],
-            jnp.zeros((4, LANES), jnp.float32),
+            jnp.zeros((EDGE - SLABS - 4, LANES), jnp.float32),
         ], axis=0)
         if k:
             value = value + edges[2 * levels + k - 1] * sums[-1]
@@ -612,17 +612,18 @@
     lane = lane_of((GROUPS, LANES))
     slab = row_of((GROUPS, LANES))
     for k in range(levels):
-        if k % per == 0:
-            copies[k // per].wait()
         west = sums[k][0:GROUPS]
-        east = turn(sums[k][SLABS : SLABS + GROUPS], -17)
-        south_l, south_r = sums[k][48:49], sums[k][49:50]
-        north_l, north_r = turn(sums[k][50:51], 16), turn(sums[k][51:52], 16)
+        east = turn(west, -18)
+        south_l, south_r = sums[k][SLABS : SLABS + 1], sums[k][SLABS + 1 : SLABS + 2]
+        north_l = turn(sums[k][SLABS + 2 : SLABS + 3], 16)
+        north_r = turn(sums[k][SLABS + 3 : SLABS + 4], 16)
         for a in range(PLANES):
             rim = None
             for at, source in [(at, west) for at in FIRST_OF[a]] + [(at, east) for at in LAST_OF[a]]:
                 rim = jnp.where(lane == at, source, 0.0 if rim is None else rim)
+            rows = comb(k * ROWS + a)
             if rim is None:
+                cells[rows, :] = inner[rows, :]
                 continue
             if a == 0:
                 rim = rim + jnp.where(slab == 0, south_l, 0.0)
@@ -632,8 +633,7 @@
                 rim = rim + jnp.where(jnp.logical_and(slab == GROUPS - 1, lane >= 16), north_l, 0.0)
             if a == PLANES - 1:
                 rim = rim + jnp.where(slab == GROUPS - 1, jnp.where(lane < 16, north_l, north_r), 0.0)
-            rows = comb(k * ROWS + a)
-            cells[rows, :] = cells[rows, :] + rim
+            cells[rows, :] = inner[rows, :] + rim
         if k % per == per - 1:
             step = k // per
             copy = pltpu.make_async_copy(
@@ -647,9 +647,9 @@
 
 def tracer_kernel(
     levels, per, temp_in, zonal_in, merid_in, rates_in, ocean_in,
-    inner_out, edges_out,
-    temp, zonal, merid, rates, ocean, out, edges,
-    te, tw, tn, ts, stepped, border, sems, out_sems,
+    out, edges,
+    temp, zonal, merid, rates, ocean,
+    te, tw, tn, ts, stepped, border, sems,
 ):
     steps = levels // per
     pairs = [(ocean_in.reshape(ROWS, LANES), ocean)]
@@ -719,12 +719,13 @@
         def get(a):
             return ref[comb(base + a), :].astype(jnp.float32)
 
-        border[0:GROUPS] = choose(START, lane, get)
-        border[SLABS : SLABS + GROUPS] = turn(choose(LAST, lane, get), 17)
-        border[48:50] = ref[base : base + 2, :].astype(jnp.float32)
+        border[0:GROUPS] = jnp.where(
+            lane % 16 == 1, turn(choose(LAST, lane, get), 18), choose(START, lane, get)
+        )
+        border[SLABS : SLABS + 2] = ref[base : base + 2, :].astype(jnp.float32)
         rows = ref[base + ROWS - 2 : base + ROWS, :].astype(jnp.float32)
-        border[50:51] = turn(jnp.where(one >= 16, rows[0:1], rows[1:2]), -16)
-        border[51:52] = turn(rows[1:2], -16)
+        border[SLABS + 2 : SLABS + 3] = turn(jnp.where(one >= 16, rows[0:1], rows[1:2]), -16)
+        border[SLABS + 3 : SLABS + 4] = turn(rows[1:2], -16)
         edges[at] = border[...]
 
     border[...] = jnp.zeros_like(border)
@@ -744,12 +745,6 @@
         else:
             inverse = 1.0 / pivot
         edges[levels - 1 + k] = inverse
-        if k == 0:
-            results = fetching([(out, inner_out)], out_sems)
-    results.append(pltpu.make_async_copy(edges, edges_out, out_sems.at[1]))
-    results[-1].start()
-    for copy in results:
-        copy.wait()
 
 
 def on_device(
@@ -773,6 +768,7 @@
     per = next(n for n in (4, 2, 6, levels) if levels % n == 0 and n * ROWS % 8 == 0)
     steps = levels // per
     large = pltpu.CompilerParams(vmem_limit_bytes=BUDGET)
+    middle = pltpu.CompilerParams(vmem_limit_bytes=BUDGET * 7 // 8)
     small = pltpu.CompilerParams(vmem_limit_bytes=BUDGET // 3)
     temp, zonal, merid = (
         array.reshape(levels * ROWS, LANES)
@@ -820,13 +816,12 @@
     inner, edges = pl.pallas_call(
         functools.partial(tracer_kernel, levels, per),
         in_specs=[hbm] * 5,
-        out_specs=[hbm] * 2,
+        out_specs=[here] * 2,
         out_shape=[out(levels * ROWS, LANES), out(3 * levels - 1, EDGE, LANES)],
-        scratch_shapes=[deep] * 3 + [vmem((levels - 1) * ROWS, LANES), flat_int, deep]
-        + [vmem(3 * levels - 1, EDGE, LANES)]
+        scratch_shapes=[deep] * 3 + [vmem((levels - 1) * ROWS, LANES), flat_int]
         + [plane] * 2 + [tall] * 2
-        + [vmem(levels, PLANES, GROUPS, LANES), vmem(EDGE, LANES), sems(3 * steps + 2), sems(2)],
-        compiler_params=large,
+        + [vmem(levels, PLANES, GROUPS, LANES), vmem(EDGE, LANES), sems(3 * steps + 2)],
+        compiler_params=middle,
         name="tracer",
     )(temp, zonal, merid, rates, ocean)
 
@@ -845,13 +840,12 @@
 
     new_temp, surface = pl.pallas_call(
         functools.partial(finish_kernel, levels, per),
-        in_specs=[SMEM] + [here] * 3 + [hbm],
+        in_specs=[SMEM] + [here] * 4,
         out_specs=[hbm] * 2,
         out_shape=[out(levels * ROWS, LANES), out(1, cells)],
-        input_output_aliases={4: 0},
         scratch_shapes=[
             deep, flat, vmem(GROUP, SLABS, LANES), vmem(GROUP, SLABS, LANES), vmem(4, 2 * levels, LANES),
-            sems(steps), sems(1 + steps),
+            sems(1 + steps),
         ],
         compiler_params=small,
         name="finish",

time: 43.4 us -> 42.8 us (0.986)
  Pallas kernels: 20.1 us -> 18.1 us
  local copies, waits for them, and re-layouts: 0.04 us -> 1.47 us
    unnamed x16, local copies, waits for them, and re-layouts: 0.04 us -> 1.47 us
    pallas_call x1, Pallas kernels: 9.01 us -> 7.64 us  [on_device(): pl.pallas_call(functools.partial(tracer_kernel, levels, per), in_specs=[h...]
    pallas_call x1, Pallas kernels: 3.12 us -> 2.36 us  [on_device(): pl.pallas_call(functools.partial(finish_kernel, levels, per), in_specs=[S...]
  transfers between devices with their start and end apart: 1 -> 1, of which waited for: 1 -> 1; matrix products, arithmetic and copies ran while one was open for 0% -> 0% of each run, Pallas kernels for 21% -> 18%
where the time goes in v1:
time: 42.8 us; the launch traced here: 42.5 us
  Pallas kernels  18.1 us (42%)
  blocking collectives  11.2 us (26%)
  starting transfers between devices  7.3 us (17%)
  waiting for transfers between devices  3.64 us (9%)
  local copies, waits for them, and re-layouts  1.47 us (3%)
  between operations  0.73 us (2%)
    all_to_all x1, blocking collectives, on_device(): hands = lax.all_to_all(hand, BOTH, 0, 0, tiled=True)  11.2 us
    pallas_call x1, Pallas kernels, on_device(): pl.pallas_call(functools.partial(tracer_kernel, levels, per), in_specs=[h...  7.64 us
    all_to_all x1, starting transfers between devices, on_device(): rims = lax.all_to_all(slots, BOTH, 0, 0, tiled=True)  7.3 us
    pallas_call x1, Pallas kernels, on_device(): pl.pallas_call(functools.partial(forcing_kernel, levels, per, nx, ny), in...  5.59 us
    all_to_all x1, waiting for transfers between devices, on_device(): rims = lax.all_to_all(slots, BOTH, 0, 0, tiled=True)  3.64 us
    pallas_call x1, Pallas kernels, on_device(): pl.pallas_call(functools.partial(solve_kernel, levels, ny), in_specs=[SME...  2.53 us
    pallas_call x1, Pallas kernels, on_device(): pl.pallas_call(functools.partial(finish_kernel, levels, per), in_specs=[S...  2.36 us
    unnamed x16, local copies, waits for them, and re-layouts  1.47 us
  transfers between devices with their start and end apart: 1, of which 1 were waited for; matrix products, arithmetic and copies ran while one was open for 0% of the time, Pallas kernels for 18%

profile of v1, /device:TPU:0, one launch (start us, length us, event | category | flops | bytes accessed | tf_op | source)
XLA Modules:
  0.0 42.5 jit_solution(3486856217072005005)
XLA Ops:
  0.6 0.0 copy-start.1
  0.6 5.6 %forcing.1 = (f32[300,128]{1,0:T(8,128)}, f32[56,128]{1,0:T(8,128)}, f32[32,1,3456]{2,1,0:T(1,128)}, s32[8]{0:T(128)}, s32[128]{0:T(128)}) custom-call(s32[32]{0:T(128)} %pos.1, f32[3600,128]{1,0:T(8,128)} %bitcast.6, f32[3600,128]{1,0:T(8,128)} %bitcast.8, f32[3600,128]{1,0:T(8,128)} %bitcast.10, f32[1,38400]{1,0:T(1,128)} %depth.1, s32[1,38400]{1,0:T(1,128)} %ocean.1, ...), custom_call_target="tpu_custom_call" | custom-call | tf_op jit(solution)/shard_map/forcing/pallas_call | solution.py:799
  6.2 7.3 %all-to-all-start = ((f32[32,1,3456]{2,1,0:T(1,128)}), f32[32,1,3456]{2,1,0:T(1,128)S(1)}, u32[]{:S(2)}, u32[]{:S(2)}) async-start(f32[32,1,3456]{2,1,0:T(1,128)} %get-tuple-element.17), calls=%async_computation | async-start | bytes 884736 | tf_op jit(solution)/shard_map/all_to_all | solution.py:814
  13.6 0.0 copy-done.1
  13.6 0.0 copy-start
  13.6 1.4 %copy-done = f32[1,11,38400]{2,0,1:T(1,128)S(1)} copy-done((f32[1,11,38400]{2,0,1:T(1,128)S(1)}, f32[1,11,38400]{2,0,1:T(1,128)}, u32[]{:S(2)}) %copy-start) | copy-done | bytes 1689624
  15.0 0.0 copy-start.2
  15.0 0.0 copy-start.3
  15.0 0.0 copy-start.4
  15.0 0.0 copy-start.5
  15.0 0.0 copy-start.6
  15.0 0.0 copy-start.7
  15.0 7.6 %tracer.1 = (f32[3600,128]{1,0:T(8,128)S(1)}, f32[35,32,128]{2,1,0:T(8,128)S(1)}) custom-call(f32[3600,128]{1,0:T(8,128)} %bitcast.7, f32[3600,128]{1,0:T(8,128)} %bitcast.9, f32[3600,128]{1,0:T(8,128)} %bitcast.11, f32[11,1,38400]{2,1,0:T(1,128)S(1)} %bitcast.5, s32[1,38400]{1,0:T(1,128)S(1)} %copy-done.1), custom_call_target="tpu_custom_call" | custom-call | tf_op jit(solution)/shard_map/tracer/pallas_call | solution.py:816
  22.7 3.6 %all-to-all-done.rims = f32[32,1,3456]{2,1,0:T(1,128)S(1)} async-done(((f32[32,1,3456]{2,1,0:T(1,128)}), f32[32,1,3456]{2,1,0:T(1,128)S(1)}, u32[]{:S(2)}, u32[]{:S(2)}) %all-to-all-start) | async-done | bytes 442400 | tf_op jit(solution)/shard_map/all_to_all | solution.py:814
  26.3 0.0 copy-done.2
  26.3 0.0 copy-done.3
  26.3 0.0 copy-done.4
  26.3 0.0 copy-done.5
  26.4 0.0 copy-done.6
  26.4 0.0 copy-done.7
  26.4 2.5 %vectors.1 = (f32[4,8,24,256]{3,2,1,0:T(8,128)S(1)}, f32[32,1,512]{2,1,0:T(1,128)S(1)}) custom-call(s32[8]{0:T(128)S(1)} %copy-done.6, s32[128]{0:T(128)S(1)} %copy-done.7, f32[32,1,3456]{2,1,0:T(1,128)S(1)} %all-to-all-done.rims, f32[56,128]{1,0:T(8,128)S(1)} %copy-done.5, f32[300,128]{1,0:T(8,128)S(1)} %copy-done.4, f32[1,38400]{1,0:T(1,128)S(1)} %copy-done.2, ...), custom_call_target="tpu_custom_call" | custom-call | tf_op jit(solution)/shard_map/vectors/pallas_call | solution.py:830
  28.9 11.2 %all_to_all.10.hands = f32[32,1,512]{2,1,0:T(1,128)S(1)} all-to-all(f32[32,1,512]{2,1,0:T(1,128)S(1)} %get-tuple-element.22), channel_id=1, replica_groups=mesh['gx'=8,'gy'=4] {'gx','gy'}, dimensions={0} | all-to-all | bytes 131072 | tf_op jit(solution)/shard_map/all_to_all | solution.py:839
  40.1 2.4 %finish.1 = (f32[3600,128]{1,0:T(8,128)}, f32[1,38400]{1,0:T(1,128)}) custom-call(s32[8]{0:T(128)S(1)} %copy-done.6, f32[32,1,512]{2,1,0:T(1,128)S(1)} %all_to_all.10.hands, f32[4,8,24,256]{3,2,1,0:T(8,128)S(1)} %get-tuple-element.23.vectors, f32[35,32,128]{2,1,0:T(8,128)S(1)} %get-tuple-element.24.edges, f32[3600,128]{1,0:T(8,128)S(1)} %get-tuple-element.25.inner), custom_call_target="tpu_custom_call" | custom-call | tf_op jit(solution)/shard_map/finish/pallas_call | solution.py:841
Async XLA Ops:
  0.6 12.9 %copy-start.1 = (s32[1,38400]{1,0:T(1,128)S(1)}, s32[1,38400]{1,0:T(1,128)}, u32[]{:S(2)}) copy-start(s32[1,38400]{1,0:T(1,128)} %ocean.1) | copy-start | bytes 460804
  6.2 20.1 %all-to-all-start = ((f32[32,1,3456]{2,1,0:T(1,128)}), f32[32,1,3456]{2,1,0:T(1,128)S(1)}, u32[]{:S(2)}, u32[]{:S(2)}) async-start(f32[32,1,3456]{2,1,0:T(1,128)} %get-tuple-element.17), calls=%async_computation | async-start | bytes 884736 | tf_op jit(solution)/shard_map/all_to_all | solution.py:814
  13.6 1.5 %copy-start = (f32[1,11,38400]{2,0,1:T(1,128)S(1)}, f32[1,11,38400]{2,0,1:T(1,128)}, u32[]{:S(2)}) copy-start(f32[1,11,38400]{2,0,1:T(1,128)} %param.12) | copy-start | bytes 5068804
  15.0 11.3 %copy-start.2 = (f32[1,38400]{1,0:T(1,128)S(1)}, f32[1,38400]{1,0:T(1,128)}, u32[]{:S(2)}) copy-start(f32[1,38400]{1,0:T(1,128)} %depth.1) | copy-start | bytes 460804
  15.0 11.3 %copy-start.3 = (f32[1,38400]{1,0:T(1,128)S(1)}, f32[1,38400]{1,0:T(1,128)}, u32[]{:S(2)}) copy-start(f32[1,38400]{1,0:T(1,128)} %diag.1) | copy-start | bytes 460804
  15.0 11.3 %copy-start.4 = (f32[300,128]{1,0:T(8,128)S(1)}, f32[300,128]{1,0:T(8,128)}, u32[]{:S(2)}) copy-start(f32[300,128]{1,0:T(8,128)} %get-tuple-element.21.part) | copy-start | bytes 460804
  15.0 11.3 %copy-start.5 = (f32[56,128]{1,0:T(8,128)S(1)}, f32[56,128]{1,0:T(8,128)}, u32[]{:S(2)}) copy-start(f32[56,128]{1,0:T(8,128)} %get-tuple-element.20.own) | copy-start | bytes 86020
  15.0 11.3 %copy-start.6 = (s32[8]{0:T(128)S(1)}, s32[8]{0:T(128)}, u32[]{:S(2)}) copy-start(s32[8]{0:T(128)} %get-tuple-element.15.table) | copy-start | bytes 100
  15.0 11.3 %copy-start.7 = (s32[128]{0:T(128)S(1)}, s32[128]{0:T(128)}, u32[]{:S(2)}) copy-start(s32[128]{0:T(128)} %get-tuple-element.16.around) | copy-start | bytes 1540

commit v2 on v1

--- a/solution.py
+++ b/solution.py
@@ -35,7 +35,7 @@
 END = [(SPAN_X * j + SPAN_X - 1) % LANES for j in range(GROUP)]
 FIRST_OF = [[OFF[j] for j in range(GROUP) if START[j] == a] for a in range(PLANES)]
 LAST_OF = [[END[j] for j in range(GROUP) if LAST[j] == a] for a in range(PLANES)]
-RIM_ROWS = 24
+RIM_ROWS = 20
 EDGE = 32
 BUDGET = 56 * 1024 * 1024
 
@@ -85,6 +85,17 @@
 
 def comb(a, count=GROUPS):
     return pl.ds(a, count, stride=PLANES)
+
+
+def line_of(get, y):
+    lane = lane_of((1, LANES))
+    j = y % GROUP
+    row = y // GROUP * PLANES + START[j]
+    first, second = get(row), get(row + 1)
+    third = get(row + 2) if START[j] + 2 < PLANES else second
+    left = turn(jnp.where(lane >= OFF[j], first, second), -OFF[j])
+    right = turn(jnp.where(lane >= OFF[j], second, third), -OFF[j])
+    return left, right
 
 
 def drop(value, lanes, lane):
@@ -229,9 +240,11 @@
             k = step * per + n
             t, u, v = (flat[n] for flat in flats)
 
+            loaded = {a: (t.plane(a), u.plane(a)) for a in sorted(set(START + LAST))}
+
             def term(planes, sign):
-                own = choose(planes, lane, t.plane)
-                flow = choose(planes, lane, u.plane)
+                own = choose(planes, lane, lambda a: loaded[a][0])
+                flow = choose(planes, lane, lambda a: loaded[a][1])
                 return DIFFUSE * own + sign * ADVECT * (flow * own)
 
             edges[0, 0:GROUPS] = jnp.where(q == k, turn(term(START, -1.0), k), edges[0, 0:GROUPS])
@@ -269,34 +282,37 @@
         part[comb(a), :] = source[comb(a), :] + (STERIC / levels) * wet * (total + wet * change)
     send(part, part_out)
 
-    def mix(values):
-        value = values[4]
-        for at, low in ((3, 12), (2, 11), (1, 8), (0, 4)):
+    def mix(*values):
+        value = values[-1]
+        for at, low in ((6, 12), (5, 11), (4, 10), (3, 9), (2, 8), (1, 6), (0, 3)):
             value = jnp.where(q < low, values[at], value)
         return value
-
-    def flat(ref):
-        return lambda a: ref[comb(a), :]
 
     def ends(planes, low):
         value = tn[planes[0], 8 : 8 + GROUPS]
         last = jnp.logical_and(lane >= low, lane < low + 16)
         return jnp.where(last, ts[planes[7], 8 : 8 + GROUPS], value)
 
-    pack_w = mix([
-        choose(START, lane, flat(part)),
-        turn(choose(START, lane, lambda a: masked(comb(a))), 4),
-        turn(choose(START, lane, flat(diag)), 8),
-        turn(choose(START, lane, lambda a: te[a]), 11),
-        turn(ends(START, OFF[7]), 12),
-    ])
-    pack_e = mix([
-        turn(choose(LAST, lane, flat(part)), 20),
-        turn(choose(LAST, lane, lambda a: masked(comb(a))), 24),
-        turn(choose(LAST, lane, flat(diag)), 27),
-        turn(choose(LAST, lane, lambda a: tw[a]), 28),
-        turn(ends(LAST, LANES - 16), 32),
-    ])
+    def beside(b, d, g, b_out, d_out):
+        return g * b + d * d_out * (b - b_out)
+
+    bp = choose(START, lane, lambda a: part[comb(a), :])
+    dp = choose(START, lane, lambda a: masked(comb(a)))
+    gp = choose(START, lane, lambda a: diag[comb(a), :])
+    pp = beside(bp, dp, gp, turn(bp, -1), turn(dp, -1))
+    pack_w = mix(
+        bp, turn(dp, 3), turn(gp, 6), turn(pp, 6), turn(choose(START, lane, lambda a: te[a]), 9),
+        turn(gp, 8), turn(dp, 8), turn(ends(START, OFF[7]), 12),
+    )
+    bp = choose(LAST, lane, lambda a: part[comb(a), :])
+    dp = choose(LAST, lane, lambda a: masked(comb(a)))
+    gp = choose(LAST, lane, lambda a: diag[comb(a), :])
+    pp = beside(bp, dp, gp, turn(bp, 1), turn(dp, 1))
+    pack_e = mix(
+        turn(bp, 19), turn(dp, 22), turn(gp, 24), turn(pp, 27),
+        turn(choose(LAST, lane, lambda a: tw[a]), 26),
+        turn(gp, 29), turn(dp, 31), turn(ends(LAST, LANES - 16), 32),
+    )
     own[0:GROUPS] = pack_w
     own[SLABS : SLABS + GROUPS] = pack_e
     north_l = tn[0, 8:9]
@@ -315,32 +331,46 @@
     top = jnp.broadcast_to(top, (1, LANES))
 
     slots[pl.ds(RIM_ROWS - 1, count, stride=slot), :] = jnp.broadcast_to(top, (count, LANES))
-    eight = lane_of((8, LANES))
-    eighth = row_of((8, LANES))
+    block_lane = lane_of((6, LANES))
+    block_row = row_of((6, LANES))
     for c, first, rows_l, rows_r in ((2, True, north_l, north_r), (3, False, south_l, south_r)):
-        base = 0 if first else ROWS - 8
-        spare = jnp.logical_and(eighth == 7, eight >= 64) if first else jnp.logical_and(eighth == 0, eight < 64)
+        base = 0 if first else ROWS - 6
+        if first:
+            spare = jnp.logical_and(block_row == 5, block_lane >= 80)
+        else:
+            spare = jnp.logical_and(block_row == 0, block_lane < 48)
         g = 0 if first else GROUPS - 1
         blocks = []
-        block = slice(base, base + 8)
+        block = slice(base, base + 6)
         for value, at in ((part[block, :], g), (masked(block), SLABS + g)):
-            extra = jnp.broadcast_to(turn(own[at : at + 1], -16), (8, LANES))
+            extra = jnp.broadcast_to(turn(own[at : at + 1], -16), (6, LANES))
             blocks.append(jnp.where(spare, extra, value))
-        low = 0 if first else ROWS - 6
-        diag_rows = diag[low : low + 6, :]
+        low = 0 if first else ROWS - 4
+        diag_rows = diag[low : low + 4, :]
+        third, fourth = (2, 3) if first else (SPAN_Y - 3, SPAN_Y - 4)
+        b_l, b_r = line_of(lambda n: part[n : n + 1, :], third)
+        d_l, d_r = line_of(lambda n: masked(slice(n, n + 1)), third)
+        g_l, g_r = line_of(lambda n: diag[n : n + 1, :], third)
+        bo_l, bo_r = line_of(lambda n: part[n : n + 1, :], fourth)
+        do_l, do_r = line_of(lambda n: masked(slice(n, n + 1)), fourth)
+        out_l = beside(b_l, d_l, g_l, bo_l, do_l)
+        out_r = beside(b_r, d_r, g_r, bo_r, do_r)
+        for at, value in ((112, turn(g_l, 112)), (113, turn(do_l, 113)), (114, turn(g_r, 3)), (115, turn(do_r, 4))):
+            out_r = jnp.where(one == at, value, out_r)
         last_row = jnp.where(one == LANES - 1, top, rows_r)
 
         @pl.when(sides[c] >= 0)
-        def _(c=c, blocks=blocks, diag_rows=diag_rows, rows_l=rows_l, last_row=last_row):
+        def _(c=c, blocks=blocks, diag_rows=diag_rows, singles=(out_l, out_r, rows_l, last_row)):
             at = sides[c] * slot
-            slots[pl.ds(at, 8), :] = blocks[0]
-            slots[pl.ds(at + 8, 8), :] = blocks[1]
-            slots[pl.ds(at + 16, 6), :] = diag_rows
-            slots[pl.ds(at + 22, 1), :] = rows_l
-            slots[pl.ds(at + 23, 1), :] = last_row
-
-    slots[pl.ds(sides[0] * slot, GROUPS), :] = pack_w
-    slots[pl.ds(sides[1] * slot, GROUPS), :] = pack_e
+            slots[pl.ds(at, 6), :] = blocks[0]
+            slots[pl.ds(at + 6, 6), :] = blocks[1]
+            slots[pl.ds(at + 12, 4), :] = diag_rows
+            for n, value in enumerate(singles):
+                slots[pl.ds(at + 16 + n, 1), :] = value
+
+    corner = jnp.logical_and(row_of((GROUPS, LANES)) == RIM_ROWS - 1, lane == LANES - 1)
+    for c, pack in ((0, pack_w), (1, pack_e)):
+        slots[pl.ds(sides[c] * slot, GROUPS), :] = jnp.where(corner, top, pack)
     for c, at in ((4, 0), (5, SLABS), (6, GROUPS - 1), (7, SLABS + GROUPS - 1)):
         @pl.when(sides[c] >= 0)
         def _(c=c, at=at):
@@ -357,7 +387,7 @@
     levels, tiles_y,
     table, around, rims, own, part, depth, ocean, diag,
     vectors, hands,
-    fb, fd, fg, pw, pe, ow, oe, ed, eg, we, wn, last, rows,
+    fb, fd, fg, pw, pe, ow, oe, ed, eg, ex, we, wn, last, rows,
 ):
     count = rims.shape[0]
     number_pieces, _ = pieces_of(levels, count)
@@ -393,16 +423,20 @@
     fb[0:ROWS] = part[...]
     fd[0:ROWS] = depth[...] * ocean[...].astype(jnp.float32)
     fg[0:ROWS] = diag[...]
-    for ref, low, high in ((fb, 0, 8), (fd, 8, 16), (fg, 16, 22)):
-        ref[ROWS : ROWS + high - low] = fetch(3, low, high)
-        ref[WIDE - high + low : WIDE] = fetch(2, low, high)
+    for ref, low, high, n_lane, s_lane in ((fb, 0, 6, 80, 48), (fd, 6, 12, 80, 48), (fg, 12, 16, 96, 32)):
+        size = high - low
+        row, column = row_of((size, LANES)), lane_of((size, LANES))
+        beyond = jnp.logical_and(row == size - 1, column >= n_lane)
+        ref[ROWS : ROWS + size] = jnp.where(beyond, 0.0, fetch(3, low, high))
+        beyond = jnp.logical_and(row == 0, column < s_lane)
+        ref[WIDE - size : WIDE] = jnp.where(beyond, 0.0, fetch(2, low, high))
     empty = jnp.zeros((SLABS, LANES), jnp.float32)
     for ref, side, north, south in ((pw, 0, 6, 4), (pe, 1, 7, 5)):
         ref[...] = empty
         ref[0:GROUPS] = fetch(side, 0, GROUPS)
         ref[GROUPS : GROUPS + 1] = fetch(north, 0, 1)
         ref[SLABS - 1 : SLABS] = fetch(south, 0, 1)
-    for ref, at, north, south in ((ow, 0, 7, 0), (oe, SLABS, 15, 8)):
+    for ref, at, north, south in ((ow, 0, 5, 0), (oe, SLABS, 11, 6)):
         ref[...] = empty
         ref[0:GROUPS] = own[at : at + GROUPS]
         ref[GROUPS : GROUPS + 1] = turn(fetch(3, north, north + 1), 16)
@@ -423,14 +457,60 @@
         return jnp.broadcast_to(left, (SLABS, LANES)), jnp.broadcast_to(right, (SLABS, LANES))
 
     seams = {
-        0: ((0, seam_row(fetch(2, 22, 23), fetch(2, 23, 24), SLABS - 1, 28)),
+        0: ((0, seam_row(fetch(2, 18, 19), fetch(2, 19, 20), SLABS - 1, 28)),
             (GROUPS, seam_row(own[50:51], own[51:52], GROUPS - 1, 28))),
-        GROUP - 1: ((GROUPS - 1, seam_row(fetch(3, 22, 23), fetch(3, 23, 24), GROUPS, 12)),
+        GROUP - 1: ((GROUPS - 1, seam_row(fetch(3, 18, 19), fetch(3, 19, 20), GROUPS, 12)),
                     (SLABS - 1, seam_row(own[48:49], own[49:50], 0, 12))),
     }
     weight = STERIC / levels
+
+    def missing(target, term, term_out, d, d_out, g):
+        term, term_out, d, d_out, g = (
+            turn(value[0], target - value[1]) for value in (term, term_out, d, d_out, g)
+        )
+        term = jnp.where(d > 0, weight * term, 0.0)
+        term_out = jnp.where(d_out > 0, weight * term_out, 0.0)
+        return jnp.where(one == target, g * term + d * d_out * (term - term_out), 0.0)
+
+    def ring(ref, at):
+        return ref[at : at + 1]
+
+    outer = {j: [] for j in range(GROUP)}
+    for j, at, beyond, o, lanes in ((0, 0, SLABS - 1, 0, 28), (GROUP - 1, GROUPS - 1, GROUPS, 16, 12)):
+        own_row, corner = ring(pe, at), ring(pe, beyond)
+        outer[j].append((1, at, missing(
+            114, (corner, lanes + 2), (corner, lanes + 3), (own_row, o + 5), (own_row, o + 11), (own_row, o + 10),
+        )))
+        own_row, corner = ring(pw, at), ring(pw, beyond)
+        outer[j].append((1, at, missing(
+            125, (corner, lanes + 1), (corner, lanes), (own_row, o + 3), (own_row, o + 11), (own_row, o + 10),
+        )))
+    for j, at, c, j_out, d_l, d_r in ((2, GROUPS, 3, 3, (9, 96), (11, 79)), (5, SLABS - 1, 2, 4, (6, 48), (8, 31))):
+        line_l, line_r = fetch(c, 16, 17), fetch(c, 17, 18)
+        corner = ring(pw, at)
+        outer[j].append((0, at, line_l + missing(
+            0, (corner, OFF[j] + 9), (corner, OFF[j_out] + 9), (fetch(c, d_l[0], d_l[0] + 1), d_l[1]),
+            (line_r, 113), (line_r, 112),
+        )))
+        corner = ring(pe, at)
+        outer[j].append((1, at, jnp.where(one < 112, line_r, 0.0) + missing(
+            111, (corner, OFF[j] + 9), (corner, OFF[j_out] + 9), (fetch(c, d_r[0], d_r[0] + 1), d_r[1]),
+            (line_r, 115), (line_r, 114),
+        )))
     for j in range(GROUP):
         o = OFF[j]
+        inside = slab < GROUPS
+        halves = [
+            jnp.zeros((SLABS, LANES), jnp.float32),
+            jnp.where(
+                jnp.logical_and(inside, lane == 114), turn(pe[...], 114 - o - 8),
+                jnp.where(jnp.logical_and(inside, lane == 125), turn(pw[...], 125 - o - 8), 0.0),
+            ),
+        ]
+        for half, at, line in outer[j]:
+            halves[half] = halves[half] + jnp.where(slab == at, line, 0.0)
+        ex[j, :, 0:LANES] = halves[0]
+        ex[j, :, LANES:] = halves[1]
 
         def rim(right, q, width):
             east = turn(pe[...], 112 - o - q)
@@ -439,20 +519,20 @@
             return jnp.where(lane < 112, right, value)
 
         left, right = spread(fd, j)
-        right = rim(right, 4, 4)
+        right = rim(right, 3, 3)
         wet_l = jnp.where(left > 0, weight, 0.0)
         wet_r = jnp.where(right > 0, weight, 0.0)
         ed[j, :, 0:LANES] = left
         ed[j, :, LANES:] = right
         left, right = spread(fg, j)
         eg[j, :, 0:LANES] = left
-        eg[j, :, LANES:] = rim(right, 8, 3)
+        eg[j, :, LANES:] = rim(right, 6, 2)
         left, right = spread(fb, j)
-        right = rim(right, 0, 4)
-        seam_l = jnp.where(lane == 0, turn(pw[...], -o - 11), 0.0)
-        seam_r = jnp.where(lane == 127, turn(ow[...], 127 - o - 11), 0.0)
-        seam_r = jnp.where(lane == 111, turn(pe[...], 111 - o - 11), seam_r)
-        seam_r = jnp.where(lane == 112, turn(oe[...], 112 - o - 11), seam_r)
+        right = rim(right, 0, 3)
+        seam_l = jnp.where(lane == 0, turn(pw[...], -o - 9), 0.0)
+        seam_r = jnp.where(lane == 127, turn(ow[...], 127 - o - 9), 0.0)
+        seam_r = jnp.where(lane == 111, turn(pe[...], 111 - o - 9), seam_r)
+        seam_r = jnp.where(lane == 112, turn(oe[...], 112 - o - 9), seam_r)
         for at, (row_l, row_r) in seams.get(j, ()):
             seam_l = seam_l + jnp.where(slab == at, row_l, 0.0)
             seam_r = seam_r + jnp.where(slab == at, row_r, 0.0)
@@ -486,6 +566,8 @@
                 flow_x = we[j] * (here - turn(here, -1))
                 flow_y = wn[j] * (here - above)
                 image = eg[j] * here + (flow_x - turn(flow_x, 1)) + (flow_y - flow_below)
+                if k == 1:
+                    image = image + ex[j]
                 fresh = scale * image - (STRETCH * ROOTS[k - 1]) * here
                 flow_below = flow_y
                 new[j] = fresh
@@ -767,6 +849,7 @@
     f32 = jnp.float32
     per = next(n for n in (4, 2, 6, levels) if levels % n == 0 and n * ROWS % 8 == 0)
     steps = levels // per
+    few = next(n for n in (2, 4, 6, levels) if levels % n == 0 and n * ROWS % 8 == 0)
     large = pltpu.CompilerParams(vmem_limit_bytes=BUDGET)
     middle = pltpu.CompilerParams(vmem_limit_bytes=BUDGET * 7 // 8)
     small = pltpu.CompilerParams(vmem_limit_bytes=BUDGET // 3)
@@ -797,7 +880,7 @@
     slot = RIM_ROWS + number_pieces
     share = 1 + number_pieces
     part, own, slots, table, around = pl.pallas_call(
-        functools.partial(forcing_kernel, levels, per, nx, ny),
+        functools.partial(forcing_kernel, levels, few, nx, ny),
         in_specs=[SMEM] + [hbm] * 7,
         out_specs=[hbm] * 3 + [SMEM] * 2,
         out_shape=[
@@ -807,7 +890,7 @@
         scratch_shapes=[deep] * 3 + [flat, flat_int, flat, flat]
         + [flat, vmem(56, LANES), vmem(count * slot, LANES)]
         + [flat] * 3 + [plane] * 3 + [tall] * 2
-        + [vmem(4, 2 * levels, LANES), numbers, sems(3 * steps + 4), sems(3)],
+        + [vmem(4, 2 * levels, LANES), numbers, sems(3 * (levels // few) + 4), sems(3)],
         compiler_params=large,
         name="forcing",
     )(block_positions, temp, zonal, merid, depth, ocean, diag, source)
@@ -832,7 +915,7 @@
         in_specs=[SMEM, SMEM] + [here] * 6,
         out_specs=[here] * 2,
         out_shape=[out(4, GROUP, SLABS, 2 * LANES), out(count, 1, share * LANES)],
-        scratch_shapes=[vmem(WIDE, LANES)] * 3 + [vmem(SLABS, LANES)] * 4 + [extended] * 5 + [vmem(16, LANES)],
+        scratch_shapes=[vmem(WIDE, LANES)] * 3 + [vmem(SLABS, LANES)] * 4 + [extended] * 6 + [vmem(16, LANES)],
         compiler_params=small,
         name="vectors",
     )(table, around, rims, own, part, depth, ocean, diag)

time: 42.8 us -> 47.8 us (1.12)
  local copies, waits for them, and re-layouts: 1.47 us -> 7.18 us
  waiting for transfers between devices: 3.64 us -> 2.22 us
  Pallas kernels: 18.1 us -> 18.8 us
    unnamed x16 -> x22, local copies, waits for them, and re-layouts: 1.47 us -> 7.18 us
    all_to_all x1, waiting for transfers between devices: 3.64 us -> 2.22 us  [on_device(): rims = lax.all_to_all(slots, BOTH, 0, 0, tiled=True)]
    pallas_call x1, Pallas kernels: 2.53 us -> 3.08 us  [on_device(): pl.pallas_call(functools.partial(solve_kernel, levels, ny), in_specs=[SME...]
  transfers between devices with their start and end apart: 1 -> 1, of which waited for: 1 -> 1; matrix products, arithmetic and copies ran while one was open for 0% -> 0% of each run, Pallas kernels for 18% -> 16%
where the time goes in v2:
time: 47.8 us; the launch traced here: 47.4 us
  Pallas kernels  18.8 us (39%)
  blocking collectives  11.1 us (23%)
  starting transfers between devices  7.42 us (16%)
  local copies, waits for them, and re-layouts  7.18 us (15%)
  waiting for transfers between devices  2.22 us (5%)
  between operations  0.7 us (1%)
    all_to_all x1, blocking collectives, on_device(): hands = lax.all_to_all(hand, BOTH, 0, 0, tiled=True)  11.1 us
    pallas_call x1, Pallas kernels, on_device(): pl.pallas_call(functools.partial(tracer_kernel, levels, per), in_specs=[h...  7.6 us
    all_to_all x1, starting transfers between devices, on_device(): rims = lax.all_to_all(slots, BOTH, 0, 0, tiled=True)  7.42 us
    unnamed x22, local copies, waits for them, and re-layouts  7.18 us
    pallas_call x1, Pallas kernels, on_device(): pl.pallas_call(functools.partial(forcing_kernel, levels, few, nx, ny), in...  5.76 us
    pallas_call x1, Pallas kernels, on_device(): pl.pallas_call(functools.partial(solve_kernel, levels, ny), in_specs=[SME...  3.08 us
    pallas_call x1, Pallas kernels, on_device(): pl.pallas_call(functools.partial(finish_kernel, levels, per), in_specs=[S...  2.36 us
    all_to_all x1, waiting for transfers between devices, on_device(): rims = lax.all_to_all(slots, BOTH, 0, 0, tiled=True)  2.22 us
  transfers between devices with their start and end apart: 1, of which 1 were waited for; matrix products, arithmetic and copies ran while one was open for 0% of the time, Pallas kernels for 16%

profile of v2, /device:TPU:0, one launch (start us, length us, event | category | flops | bytes accessed | tf_op | source)
XLA Modules:
  0.0 47.4 jit_solution(11535823532730040405)
XLA Ops:
  0.6 0.0 copy-start
  0.6 5.8 %forcing.1 = (f32[300,128]{1,0:T(8,128)}, f32[56,128]{1,0:T(8,128)}, f32[32,1,2944]{2,1,0:T(1,128)}, s32[8]{0:T(128)}, s32[128]{0:T(128)}) custom-call(s32[32]{0:T(128)} %pos.1, f32[3600,128]{1,0:T(8,128)} %bitcast.6, f32[3600,128]{1,0:T(8,128)} %bitcast.8, f32[3600,128]{1,0:T(8,128)} %bitcast.10, f32[1,38400]{1,0:T(1,128)} %depth.1, s32[1,38400]{1,0:T(1,128)} %ocean.1, ...), custom_call_target="tpu_custom_call" | custom-call | tf_op jit(solution)/shard_map/forcing/pallas_call | solution.py:882
  6.4 7.4 %all-to-all-start = ((f32[32,1,2944]{2,1,0:T(1,128)}), f32[32,1,2944]{2,1,0:T(1,128)}, u32[]{:S(2)}, u32[]{:S(2)}) async-start(f32[32,1,2944]{2,1,0:T(1,128)} %get-tuple-element.17), calls=%async_computation | async-start | bytes 753664 | tf_op jit(solution)/shard_map/all_to_all | solution.py:897
  13.8 0.0 copy-done
  13.8 0.0 copy-start.1
  13.9 0.9 %copy-done.1 = s32[1,38400]{1,0:T(1,128)S(1)} copy-done((s32[1,38400]{1,0:T(1,128)S(1)}, s32[1,38400]{1,0:T(1,128)}, u32[]{:S(2)}) %copy-start.1) | copy-done | bytes 153624
  14.8 0.0 copy-start.9
  14.8 0.0 copy-start.10
  14.8 7.6 %tracer.1 = (f32[3600,128]{1,0:T(8,128)S(1)}, f32[35,32,128]{2,1,0:T(8,128)S(1)}) custom-call(f32[3600,128]{1,0:T(8,128)} %bitcast.7, f32[3600,128]{1,0:T(8,128)} %bitcast.9, f32[3600,128]{1,0:T(8,128)} %bitcast.11, f32[11,1,38400]{2,1,0:T(1,128)S(1)} %bitcast.5, s32[1,38400]{1,0:T(1,128)S(1)} %copy-done.1), custom_call_target="tpu_custom_call" | custom-call | tf_op jit(solution)/shard_map/tracer/pallas_call | solution.py:899
  22.4 0.0 copy-start.5
  22.4 0.8 %copy-done.5 = f32[35,32,128]{2,1,0:T(8,128)} copy-done((f32[35,32,128]{2,1,0:T(8,128)}, f32[35,32,128]{2,1,0:T(8,128)S(1)}, u32[]{:S(2)}) %copy-start.5) | copy-done | bytes 573464
  23.2 2.2 %all-to-all-done.rims = f32[32,1,2944]{2,1,0:T(1,128)} async-done(((f32[32,1,2944]{2,1,0:T(1,128)}), f32[32,1,2944]{2,1,0:T(1,128)}, u32[]{:S(2)}, u32[]{:S(2)}) %all-to-all-start) | async-done | bytes 376864 | tf_op jit(solution)/shard_map/all_to_all | solution.py:897
  25.4 0.0 copy-done.9
  25.4 0.0 copy-done.10
  25.4 0.0 copy-start.2
  25.4 0.9 %copy-done.2 = s32[1,38400]{1,0:T(1,128)S(1)} copy-done((s32[1,38400]{1,0:T(1,128)S(1)}, s32[1,38400]{1,0:T(1,128)}, u32[]{:S(2)}) %copy-start.2) | copy-done | bytes 153624
  26.3 0.9 %copy-done.3 = f32[1,38400]{1,0:T(1,128)S(1)} copy-done((f32[1,38400]{1,0:T(1,128)S(1)}, f32[1,38400]{1,0:T(1,128)}, u32[]{:S(2)}) %copy-start.3) | copy-done | bytes 153624
  27.2 0.9 %copy-done.4 = f32[1,38400]{1,0:T(1,128)S(1)} copy-done((f32[1,38400]{1,0:T(1,128)S(1)}, f32[1,38400]{1,0:T(1,128)}, u32[]{:S(2)}) %copy-start.4) | copy-done | bytes 153624
  28.1 0.9 %copy-done.7 = f32[300,128]{1,0:T(8,128)S(1)} copy-done((f32[300,128]{1,0:T(8,128)S(1)}, f32[300,128]{1,0:T(8,128)}, u32[]{:S(2)}) %copy-start.7) | copy-done | bytes 153624
  29.1 0.7 %copy-done.8 = f32[56,128]{1,0:T(8,128)S(1)} copy-done((f32[56,128]{1,0:T(8,128)S(1)}, f32[56,128]{1,0:T(8,128)}, u32[]{:S(2)}) %copy-start.8) | copy-done | bytes 28696
  29.8 3.1 %vectors.1 = (f32[4,8,24,256]{3,2,1,0:T(8,128)S(1)}, f32[32,1,512]{2,1,0:T(1,128)S(1)}) custom-call(s32[8]{0:T(128)S(1)} %copy-done.9, s32[128]{0:T(128)S(1)} %copy-done.10, f32[32,1,2944]{2,1,0:T(1,128)} %all-to-all-done.rims, f32[56,128]{1,0:T(8,128)S(1)} %copy-done.8, f32[300,128]{1,0:T(8,128)S(1)} %copy-done.7, f32[1,38400]{1,0:T(1,128)S(1)} %copy-done.3, ...), custom_call_target="tpu_custom_call" | custom-call | tf_op jit(solution)/shard_map/vectors/pallas_call | solution.py:913
  32.9 11.1 %all_to_all.10.hands = f32[32,1,512]{2,1,0:T(1,128)S(1)} all-to-all(f32[32,1,512]{2,1,0:T(1,128)S(1)} %get-tuple-element.22), channel_id=1, replica_groups=mesh['gx'=8,'gy'=4] {'gx','gy'}, dimensions={0} | all-to-all | bytes 131072 | tf_op jit(solution)/shard_map/all_to_all | solution.py:922
  43.9 1.1 %copy-done.6 = f32[35,32,128]{2,1,0:T(8,128)S(1)} copy-done((f32[35,32,128]{2,1,0:T(8,128)S(1)}, f32[35,32,128]{2,1,0:T(8,128)}, u32[]{:S(2)}) %copy-start.6) | copy-done | bytes 573464
  45.0 2.4 %finish.1 = (f32[3600,128]{1,0:T(8,128)}, f32[1,38400]{1,0:T(1,128)}) custom-call(s32[8]{0:T(128)S(1)} %copy-done.9, f32[32,1,512]{2,1,0:T(1,128)S(1)} %all_to_all.10.hands, f32[4,8,24,256]{3,2,1,0:T(8,128)S(1)} %get-tuple-element.23.vectors, f32[35,32,128]{2,1,0:T(8,128)S(1)} %copy-done.6, f32[3600,128]{1,0:T(8,128)S(1)} %get-tuple-element.25.inner), custom_call_target="tpu_custom_call" | custom-call | tf_op jit(solution)/shard_map/finish/pallas_call | solution.py:924
  (5 shorter events, 0.0 us)
Async XLA Ops:
  0.6 13.2 %copy-start = (f32[1,11,38400]{2,0,1:T(1,128)S(1)}, f32[1,11,38400]{2,0,1:T(1,128)}, u32[]{:S(2)}) copy-start(f32[1,11,38400]{2,0,1:T(1,128)} %param.12) | copy-start | bytes 5068804
  6.4 19.0 %all-to-all-start = ((f32[32,1,2944]{2,1,0:T(1,128)}), f32[32,1,2944]{2,1,0:T(1,128)}, u32[]{:S(2)}, u32[]{:S(2)}) async-start(f32[32,1,2944]{2,1,0:T(1,128)} %get-tuple-element.17), calls=%async_computation | async-start | bytes 753664 | tf_op jit(solution)/shard_map/all_to_all | solution.py:897
  13.8 0.9 %copy-start.1 = (s32[1,38400]{1,0:T(1,128)S(1)}, s32[1,38400]{1,0:T(1,128)}, u32[]{:S(2)}) copy-start(s32[1,38400]{1,0:T(1,128)} %ocean.1) | copy-start | bytes 460804
  14.8 10.6 %copy-start.9 = (s32[8]{0:T(128)S(1)}, s32[8]{0:T(128)}, u32[]{:S(2)}) copy-start(s32[8]{0:T(128)} %get-tuple-element.15.table) | copy-start | bytes 100
  14.8 10.6 %copy-start.10 = (s32[128]{0:T(128)S(1)}, s32[128]{0:T(128)}, u32[]{:S(2)}) copy-start(s32[128]{0:T(128)} %get-tuple-element.16.around) | copy-start | bytes 1540
  22.4 0.8 %copy-start.5 = (f32[35,32,128]{2,1,0:T(8,128)}, f32[35,32,128]{2,1,0:T(8,128)S(1)}, u32[]{:S(2)}) copy-start(f32[35,32,128]{2,1,0:T(8,128)S(1)} %get-tuple-element.24.edges) | copy-start | bytes 1720324
  25.4 0.9 %copy-start.2 = (s32[1,38400]{1,0:T(1,128)S(1)}, s32[1,38400]{1,0:T(1,128)}, u32[]{:S(2)}) copy-start(s32[1,38400]{1,0:T(1,128)} %ocean.1) | copy-start | bytes 460804
  26.3 0.9 %copy-start.3 = (f32[1,38400]{1,0:T(1,128)S(1)}, f32[1,38400]{1,0:T(1,128)}, u32[]{:S(2)}) copy-start(f32[1,38400]{1,0:T(1,128)} %depth.1) | copy-start | bytes 460804
  27.2 0.9 %copy-start.4 = (f32[1,38400]{1,0:T(1,128)S(1)}, f32[1,38400]{1,0:T(1,128)}, u32[]{:S(2)}) copy-start(f32[1,38400]{1,0:T(1,128)} %diag.1) | copy-start | bytes 460804
  28.1 0.9 %copy-start.7 = (f32[300,128]{1,0:T(8,128)S(1)}, f32[300,128]{1,0:T(8,128)}, u32[]{:S(2)}) copy-start(f32[300,128]{1,0:T(8,128)} %get-tuple-element.21.part) | copy-start | bytes 460804
  29.1 0.7 %copy-start.8 = (f32[56,128]{1,0:T(8,128)S(1)}, f32[56,128]{1,0:T(8,128)}, u32[]{:S(2)}) copy-start(f32[56,128]{1,0:T(8,128)} %get-tuple-element.20.own) | copy-start | bytes 86020
  43.9 1.1 %copy-start.6 = (f32[35,32,128]{2,1,0:T(8,128)S(1)}, f32[35,32,128]{2,1,0:T(8,128)}, u32[]{:S(2)}) copy-start(f32[35,32,128]{2,1,0:T(8,128)} %copy-done.5) | copy-start | bytes 1720324
